TPU v7x, 128 devices: a whole 4x4x4 slice. The times are simulated.
128 devices in a mesh: amp: 16 (over y, z), blk: 8 (over x, core).
Axes of the slice: x: 4, y: 4, z: 4, core: 2. Of those that a mesh axis runs over, the one named last changes fastest.
Arguments:
- pixels: float32 [1048576, 512], P(('amp', 'blk')), may hold values from -24 to 24, as said below
- sketch: float32 [512, 128], replicated, may hold values from -0.25 to 0.25
Outputs:
- basis: float32 [1048576, 128], P(('amp', 'blk'))
- coefficients: float32 [512, 128], replicated
Inputs may be any that keep to these rules, and one draw needn't show every extreme that they name: `pixels`: pixel values, finite.
All inputs are finite; a program needn't handle non-finite values.
Results may differ from a plain program's by a relative error of at most 0.0003.
Values sent between devices are 32-bit elements; how exact they have to be, the bound alone decides.
No kernel may reach another device: no remote copies, remote signals or barrier semaphores. Data moves between devices by JAX's collectives and lax.ppermute only.
A program may use at most 128 MiB of HBM per device.

v0:
```python
import jax
import jax.numpy as jnp
from jax import lax
from jax.sharding import PartitionSpec as P

POWER = 3


def total(stacked):
    return lax.psum(stacked, ("amp", "blk"))


def factor(gram_block, cross_block):
    lower_factor = jnp.linalg.cholesky(gram_block)
    mixed = jax.scipy.linalg.solve_triangular(lower_factor, cross_block.T, lower=True).T
    return (lower_factor, mixed)


def body(pixels, sketch):
    high = lax.Precision.HIGHEST
    rank = sketch.shape[1]
    pixel_count = pixels.shape[0] * lax.axis_size("amp") * lax.axis_size("blk")
    lower_factor = None
    mixed = None
    current = jnp.dot(pixels, sketch, precision=high, preferred_element_type=jnp.float32)
    for sweep in range(POWER + 1):
        gram_block = jnp.dot(current.T, current, precision=high, preferred_element_type=jnp.float32)
        cross_block = jnp.dot(pixels.T, current, precision=high, preferred_element_type=jnp.float32)
        summed = total(jnp.concatenate([gram_block, cross_block], axis=0))
        lower_factor, mixed = factor(summed[:rank], summed[rank:])
        if sweep < POWER:
            current = jnp.dot(pixels, mixed, precision=high, preferred_element_type=jnp.float32)
    scale = jnp.sqrt(jnp.asarray(pixel_count, dtype=pixels.dtype))
    coefficients = mixed / scale
    identity = jnp.eye(rank, dtype=pixels.dtype)
    inverse = jax.scipy.linalg.solve_triangular(lower_factor, identity, lower=True).T * scale
    basis = jnp.dot(current, inverse, precision=high, preferred_element_type=jnp.float32)
    return (basis, coefficients)


def solution(mesh):
    return jax.shard_map(
        body,
        mesh=mesh,
        in_specs=(P(("amp", "blk"), None), P()),
        out_specs=(P(("amp", "blk"), None), P()),
        check_vma=False,
    )
```

profile of v0, /device:TPU:1, one launch (start us, length us, event | category | flops | bytes accessed | tf_op | source)
XLA Modules:
  0.0 849.4 jit_solution(16618477288256468658)
XLA Ops:
  7.2 0.9 copy-done
  8.1 18.2 %fusion.21 = f32[8192,128]{1,0:T(8,128)S(1)} fusion(f32[8192,512]{1,0:T(8,128)} %param.5, f32[512,128]{1,0:T(8,128)S(1)} %copy-done), kind=kOutput, calls=%fused_computation.51 | convolution fusion | flops 6442450944 | bytes 21233664 | tf_op jit(solution)/shard_map/dot_general | solution.py:25
  26.3 6.9 fusion.22
  33.3 11.1 %convolution_bitcast_fusion.3 = f32[512,128]{0,1:T(8,128)S(1)} fusion(f32[8192,128]{1,0:T(8,128)S(1)} %fusion.21, f32[8192,512]{1,0:T(8,128)S(1)} %bitcast.89), kind=kOutput, calls=%fused_computation.5 | convolution fusion | flops 6442450944 | bytes 21233664 | tf_op jit(solution)/shard_map/dot_general | solution.py:28
  45.3 146.7 %all-reduce.5.cloned.1.call-done = f32[640,128]{0,1:T(8,128)} async-done(((f32[640,128]{0,1:T(8,128)}), f32[640,128]{0,1:T(8,128)}) %all-reduce.5.cloned.1.call-update) | async-done | bytes 327696 | tf_op jit(solution)/shard_map/psum | solution.py:10
  192.9 0.9 fusion.16
  193.8 11.7 %cholesky.74 = f32[128,128]{1,0:T(8,128)S(1)} custom-call(f32[128,128]{1,0:T(8,128)S(1)} %fusion.16), custom_call_target="Cholesky" | custom-call | tf_op jit(solution)/shard_map/jit(cholesky)/cholesky | solution.py:14
  206.8 9.8 %custom-call.13 = f32[1,128,128]{1,2,0:T(8,128)S(1)} custom-call(f32[1,128,128]{2,1,0:T(8,128)S(1)} %fusion.4), custom_call_target="InvertDiagBlocksLowerTriangular" | custom-call | tf_op jit(solution)/shard_map/jit(_solve_triangular)/triangular_solve | solution.py:15
  216.7 1.4 fusion.3
  218.0 20.7 %fusion.23 = f32[128,8192]{1,0:T(8,128)S(1)} fusion(f32[128,512]{1,0:T(8,128)S(1)} %fusion.3, f32[8192,512]{1,0:T(8,128)} %param.5), kind=kOutput, calls=%fused_computation.53 | convolution fusion | flops 6442450944 | bytes 21233664 | tf_op jit(solution)/shard_map/dot_general | solution.py:32
  238.8 3.4 fusion.24
  242.2 12.1 %convolution_bitcast_fusion.2 = f32[512,128]{0,1:T(8,128)S(1)} fusion(f32[128,8192]{1,0:T(8,128)S(1)} %fusion.23, f32[8192,512]{1,0:T(8,128)} %param.5), kind=kOutput, calls=%fused_computation.4 | convolution fusion | flops 6442450944 | bytes 21233664 | tf_op jit(solution)/shard_map/dot_general | solution.py:28
  255.2 141.4 %all-reduce.7.cloned.1.call-done = f32[640,128]{0,1:T(8,128)} async-done(((f32[640,128]{0,1:T(8,128)}), f32[640,128]{0,1:T(8,128)}) %all-reduce.7.cloned.1.call-update) | async-done | bytes 327696 | tf_op jit(solution)/shard_map/psum | solution.py:10
  397.5 0.9 fusion.14
  398.4 11.7 %cholesky.85 = f32[128,128]{1,0:T(8,128)S(1)} custom-call(f32[128,128]{1,0:T(8,128)S(1)} %fusion.14), custom_call_target="Cholesky" | custom-call | tf_op jit(solution)/shard_map/jit(cholesky)/cholesky | solution.py:14
  411.5 9.8 %custom-call.14 = f32[1,128,128]{1,2,0:T(8,128)S(1)} custom-call(f32[1,128,128]{2,1,0:T(8,128)S(1)} %fusion.5), custom_call_target="InvertDiagBlocksLowerTriangular" | custom-call | tf_op jit(solution)/shard_map/jit(_solve_triangular)/triangular_solve | solution.py:15
  421.3 1.4 fusion.2
  422.7 21.0 %fusion.25 = f32[128,8192]{1,0:T(8,128)S(1)} fusion(f32[128,512]{1,0:T(8,128)S(1)} %fusion.2, f32[8192,512]{1,0:T(8,128)} %param.5), kind=kOutput, calls=%fused_computation.55 | convolution fusion | flops 6442450944 | bytes 21233664 | tf_op jit(solution)/shard_map/dot_general | solution.py:32
  443.6 3.4 fusion.26
  447.1 12.1 %convolution_bitcast_fusion.1 = f32[512,128]{0,1:T(8,128)S(1)} fusion(f32[128,8192]{1,0:T(8,128)S(1)} %fusion.25, f32[8192,512]{1,0:T(8,128)} %param.5), kind=kOutput, calls=%fused_computation.3 | convolution fusion | flops 6442450944 | bytes 21233664 | tf_op jit(solution)/shard_map/dot_general | solution.py:28
  460.0 141.4 %all-reduce.9.cloned.1.call-done = f32[640,128]{0,1:T(8,128)} async-done(((f32[640,128]{0,1:T(8,128)}), f32[640,128]{0,1:T(8,128)}) %all-reduce.9.cloned.1.call-update) | async-done | bytes 327696 | tf_op jit(solution)/shard_map/psum | solution.py:10
  602.4 0.9 fusion.12
  603.2 11.7 %cholesky.96 = f32[128,128]{1,0:T(8,128)S(1)} custom-call(f32[128,128]{1,0:T(8,128)S(1)} %fusion.12), custom_call_target="Cholesky" | custom-call | tf_op jit(solution)/shard_map/jit(cholesky)/cholesky | solution.py:14
  616.3 9.8 %custom-call.15 = f32[1,128,128]{1,2,0:T(8,128)S(1)} custom-call(f32[1,128,128]{2,1,0:T(8,128)S(1)} %fusion.6), custom_call_target="InvertDiagBlocksLowerTriangular" | custom-call | tf_op jit(solution)/shard_map/jit(_solve_triangular)/triangular_solve | solution.py:15
  626.1 1.4 fusion.1
  627.5 20.8 %fusion.27 = f32[128,8192]{1,0:T(8,128)S(1)} fusion(f32[128,512]{1,0:T(8,128)S(1)} %fusion.1, f32[8192,512]{1,0:T(8,128)} %param.5), kind=kOutput, calls=%fused_computation.57 | convolution fusion | flops 6442450944 | bytes 21233664 | tf_op jit(solution)/shard_map/dot_general | solution.py:32
  648.3 3.4 fusion.28
  651.7 12.1 %convolution_bitcast_fusion = f32[512,128]{0,1:T(8,128)S(1)} fusion(f32[128,8192]{1,0:T(8,128)S(1)} %fusion.27, f32[8192,512]{1,0:T(8,128)} %param.5), kind=kOutput, calls=%fused_computation.2 | convolution fusion | flops 6442450944 | bytes 21233664 | tf_op jit(solution)/shard_map/dot_general | solution.py:28
  664.6 141.5 %all-reduce.11.cloned.1.call-done = f32[640,128]{0,1:T(8,128)} async-done(((f32[640,128]{0,1:T(8,128)}), f32[640,128]{0,1:T(8,128)}) %all-reduce.11.cloned.1.call-update) | async-done | bytes 327696 | tf_op jit(solution)/shard_map/psum | solution.py:10
  807.9 11.7 %cholesky.107 = f32[128,128]{1,0:T(8,128)S(1)} custom-call(f32[128,128]{1,0:T(8,128)S(1)} %fusion.10), custom_call_target="Cholesky" | custom-call | tf_op jit(solution)/shard_map/jit(cholesky)/cholesky | solution.py:14
  821.0 9.8 %custom-call.9 = f32[1,128,128]{1,2,0:T(8,128)S(1)} custom-call(f32[1,128,128]{2,1,0:T(8,128)S(1)} %fusion.7), custom_call_target="InvertDiagBlocksLowerTriangular" | custom-call | tf_op jit(solution)/shard_map/jit(_solve_triangular)/triangular_solve | solution.py:36
  831.1 10.1 %fusion.29 = f32[8192,128]{1,0:T(8,128)} fusion(f32[128,8192]{1,0:T(8,128)} %copy-done.1, f32[128,128]{1,0:T(8,128)S(1)} %convolution_multiply_fusion.1), kind=kOutput, calls=%fused_computation.59 | convolution fusion | flops 1610612736 | bytes 8454144 | tf_op jit(solution)/shard_map/dot_general | solution.py:37
  (50 shorter events, 14.7 us)
Async XLA Ops:
  7.2 1.0 copy-start
  7.2 184.8 %all-reduce.5.cloned.1.call-start = ((), (), s32[]{:S(2)}) async-start(), calls=%async_computation | async-start | bytes 655360 | tf_op jit(solution)/shard_map/psum | solution.py:10
  8.1 25.2 %slice-start = ((s8[16777216]{0:T(1024)(128)(4,1)}), s8[4194304]{0:T(1024)(128)(4,1)S(1)}, s32[]{:S(2)}) async-start(s8[16777216]{0:T(1024)(128)(4,1)} %bitcast.88), calls=%async_computation.4 | async-start | bytes 8388608
  8.1 25.2 %slice-start.1 = ((s8[16777216]{0:T(1024)(128)(4,1)}), s8[4194304]{0:T(1024)(128)(4,1)S(1)}, s32[]{:S(2)}) async-start(s8[16777216]{0:T(1024)(128)(4,1)} %bitcast.88), calls=%async_computation.5 | async-start | bytes 8388608
  8.1 25.2 %slice-start.2 = ((s8[16777216]{0:T(1024)(128)(4,1)}), s8[4194304]{0:T(1024)(128)(4,1)S(1)}, s32[]{:S(2)}) async-start(s8[16777216]{0:T(1024)(128)(4,1)} %bitcast.88), calls=%async_computation.6 | async-start | bytes 8388608
  26.3 7.0 slice-start.3
  45.2 351.4 %all-reduce.7.cloned.1.call-start = ((), (), s32[]{:S(2)}) async-start(), calls=%async_computation.1 | async-start | bytes 655360 | tf_op jit(solution)/shard_map/psum | solution.py:10
  255.1 346.3 %all-reduce.9.cloned.1.call-start = ((), (), s32[]{:S(2)}) async-start(), calls=%async_computation.2 | async-start | bytes 655360 | tf_op jit(solution)/shard_map/psum | solution.py:10
  459.9 346.2 %all-reduce.11.cloned.1.call-start = ((), (), s32[]{:S(2)}) async-start(), calls=%async_computation.3 | async-start | bytes 655360 | tf_op jit(solution)/shard_map/psum | solution.py:10
  648.3 3.5 copy-start.1
  831.0 10.1 %copy-start.2 = (f32[640,128]{0,1:T(8,128)S(1)}, f32[640,128]{0,1:T(8,128)}, u32[]{:S(2)}) copy-start(f32[640,128]{0,1:T(8,128)} %all-reduce.11.cloned.1.call-done) | copy-start | bytes 983044
Sparse Core Ops, SparseCore 0:
  45.3 146.6 all-reduce.4
  255.2 141.3 all-reduce.6
  460.1 141.3 all-reduce.8
  664.8 141.3 all-reduce.10
where the time goes:
time: 854 us; the launch traced here: 849 us
  waiting for transfers between devices  571 us (67%)
  matrix products  160 us (19%)
  other arithmetic  97.8 us (11%)
  between operations  14.6 us (2%)
    psum x4, waiting for transfers between devices, total(): return lax.psum(stacked, ('amp', 'blk'))  571 us
    dot_general x3, matrix products, body(): jnp.dot(pixels, mixed, precision=high, preferred_element_type=jnp.float32)  62.5 us
    another operation x12, other arithmetic, factor(): lower_factor = jnp.linalg.cholesky(gram_block)  49.6 us
    dot_general x4, matrix products, body(): jnp.dot(pixels.T, current, precision=high, preferred_element_type=jnp.flo...  47.4 us
    another operation x6, other arithmetic, factor(): jax.scipy.linalg.solve_triangular(lower_factor, cross_block.T, lower=True)  31.4 us
    dot_general x1, matrix products, body(): jnp.dot(pixels, sketch, precision=high, preferred_element_type=jnp.float32)  18.2 us
    dot_general x4, matrix products, body(): jnp.dot(current.T, current, precision=high, preferred_element_type=jnp.fl...  17.3 us
  transfers between devices with their start and end apart: 4, of which 4 were waited for; matrix products, arithmetic and copies ran while one was open for 0% of the time, Pallas kernels for 0%

commit v1 on v0

v1 whole, which is shorter than its diff:
```python
import jax
import jax.numpy as jnp
from jax import lax
from jax.experimental import pallas as pl
from jax.experimental.pallas import tpu as pltpu
from jax.sharding import PartitionSpec as P

POWER = 3
AXES = ("amp", "blk")
CHUNK = 1024
HALF = 256


def split(x):
    high = x.astype(jnp.bfloat16)
    return high, (x - high.astype(jnp.float32)).astype(jnp.bfloat16)


def dot_t(a, b):
    return lax.dot_general(a, b, (((0,), (0,)), ((), ())), preferred_element_type=jnp.float32)


def gram_kernel(x_ref, out_ref, hh_ref, hl_ref):
    step = pl.program_id(0)

    @pl.when(step == 0)
    def _():
        hh_ref[...] = jnp.zeros_like(hh_ref)
        hl_ref[...] = jnp.zeros_like(hl_ref)

    high, low = split(x_ref[...])
    left, right = high[:, :HALF], high[:, HALF:]
    hh_ref[0] += dot_t(left, left)
    hh_ref[1] += dot_t(left, right)
    hh_ref[2] += dot_t(right, right)
    hl_ref[...] += dot_t(high, low)

    @pl.when(step == pl.num_programs(0) - 1)
    def _():
        hl = hl_ref[...]
        both = hl + hl.T
        out_ref[0] = hh_ref[0] + both[:HALF, :HALF]
        out_ref[1] = hh_ref[1] + both[:HALF, HALF:]
        out_ref[2] = hh_ref[2] + both[HALF:, HALF:]


def gram(pixels):
    rows, frames = pixels.shape
    return pl.pallas_call(
        gram_kernel,
        grid=(rows // CHUNK,),
        in_specs=[pl.BlockSpec((CHUNK, frames), lambda i: (i, 0))],
        out_specs=pl.BlockSpec((3, HALF, HALF), lambda i: (0, 0, 0)),
        out_shape=jax.ShapeDtypeStruct((3, HALF, HALF), jnp.float32),
        scratch_shapes=[
            pltpu.VMEM((3, HALF, HALF), jnp.float32),
            pltpu.VMEM((frames, frames), jnp.float32),
        ],
        compiler_params=pltpu.CompilerParams(vmem_limit_bytes=48 * 2**20),
    )(pixels)


def basis_kernel(x_ref, b_ref, out_ref):
    b_high, b_low = split(b_ref[...])
    both = jnp.concatenate([b_high, b_low], axis=1)
    high, low = split(x_ref[...])
    wide = jnp.dot(high, both, preferred_element_type=jnp.float32)
    rank = out_ref.shape[1]
    out_ref[...] = wide[:, :rank] + wide[:, rank:] + jnp.dot(low, b_high, preferred_element_type=jnp.float32)


def apply_basis(pixels, matrix):
    rows, frames = pixels.shape
    rank = matrix.shape[1]
    return pl.pallas_call(
        basis_kernel,
        grid=(rows // CHUNK,),
        in_specs=[
            pl.BlockSpec((CHUNK, frames), lambda i: (i, 0)),
            pl.BlockSpec((frames, rank), lambda i: (0, 0)),
        ],
        out_specs=pl.BlockSpec((CHUNK, rank), lambda i: (i, 0)),
        out_shape=jax.ShapeDtypeStruct((rows, rank), jnp.float32),
        compiler_params=pltpu.CompilerParams(vmem_limit_bytes=48 * 2**20),
    )(pixels, matrix)


def total(blocks):
    devices = lax.axis_size("amp") * lax.axis_size("blk")
    pieces = blocks.reshape(devices, -1, 128)
    pieces = lax.all_to_all(pieces, AXES, 0, 0, tiled=True)
    piece = jnp.sum(pieces, axis=0)
    pieces = jnp.broadcast_to(piece[None], (devices,) + piece.shape)
    pieces = lax.all_to_all(pieces, AXES, 0, 0, tiled=True)
    return pieces.reshape(blocks.shape)


def factor(gram_block, cross_block):
    lower_factor = jnp.linalg.cholesky(gram_block)
    mixed = jax.scipy.linalg.solve_triangular(lower_factor, cross_block.T, lower=True).T
    return (lower_factor, mixed)


def body(pixels, sketch):
    high = lax.Precision.HIGHEST
    rank = sketch.shape[1]
    pixel_count = pixels.shape[0] * lax.axis_size("amp") * lax.axis_size("blk")
    summed = total(gram(pixels))
    square = jnp.concatenate(
        [
            jnp.concatenate([summed[0], summed[1]], axis=1),
            jnp.concatenate([summed[1].T, summed[2]], axis=1),
        ],
        axis=0,
    )
    mixed = sketch
    lower_factor = None
    start = None
    for _ in range(POWER + 1):
        start = mixed
        cross_block = jnp.dot(square, start, precision=high, preferred_element_type=jnp.float32)
        gram_block = jnp.dot(start.T, cross_block, precision=high, preferred_element_type=jnp.float32)
        lower_factor, mixed = factor(gram_block, cross_block)
    scale = jnp.sqrt(jnp.asarray(pixel_count, dtype=pixels.dtype))
    coefficients = mixed / scale
    identity = jnp.eye(rank, dtype=pixels.dtype)
    inverse = jax.scipy.linalg.solve_triangular(lower_factor, identity, lower=True).T * scale
    matrix = jnp.dot(start, inverse, precision=high, preferred_element_type=jnp.float32)
    return (apply_basis(pixels, matrix), coefficients)


def solution(mesh):
    return jax.shard_map(
        body,
        mesh=mesh,
        in_specs=(P(AXES, None), P()),
        out_specs=(P(AXES, None), P()),
        check_vma=False,
    )
```

time: 854 us -> 186 us (0.22)
  waiting for transfers between devices: 571 us -> 0 us
  matrix products: 160 us -> 8.46 us
  blocking collectives: 0 us -> 54.1 us
  Pallas kernels: 0 us -> 24.8 us
  between operations: 14.6 us -> 1.35 us
    psum x4 -> x0, waiting for transfers between devices: 571 us -> none  [total(): return lax.psum(stacked, ('amp', 'blk'))]
    dot_general x13 -> x9, matrix products: 155 us -> 6.54 us  [the longest x4 4.2 us: body(): jnp.dot(square, start, precision=high, preferred_element_type=jnp.float32)]
    all_to_all x0 -> x2, blocking collectives: none -> 54.1 us  [total(): pieces = lax.all_to_all(pieces, AXES, 0, 0, tiled=True)]
    pallas_call x0 -> x2, Pallas kernels: none -> 24.8 us  [the longest x1 12.9 us: gram(): pl.pallas_call(gram_kernel, grid=(rows // CHUNK,), in_specs=[pl.BlockSpec...]
  transfers between devices with their start and end apart: 4 -> 0, of which waited for: 4 -> 0; matrix products, arithmetic and copies ran while one was open for 0% -> 0% of each run, Pallas kernels for 0% -> 0%
where the time goes in v1:
time: 186 us; the launch traced here: 182 us
  other arithmetic  91.8 us (49%)
  blocking collectives  54.1 us (29%)
  Pallas kernels  24.8 us (13%)
  matrix products  8.46 us (5%)
    all_to_all x2, blocking collectives, total(): pieces = lax.all_to_all(pieces, AXES, 0, 0, tiled=True)  54.1 us
    another operation x12, other arithmetic, factor(): lower_factor = jnp.linalg.cholesky(gram_block)  49.7 us
    another operation x6, other arithmetic, factor(): jax.scipy.linalg.solve_triangular(lower_factor, cross_block.T, lower=True)  31.4 us
    pallas_call x1, Pallas kernels, gram(): pl.pallas_call(gram_kernel, grid=(rows // CHUNK,), in_specs=[pl.BlockSpec...  12.9 us
    pallas_call x1, Pallas kernels, apply_basis(): pl.pallas_call(basis_kernel, grid=(rows // CHUNK,), in_specs=[pl.BlockSpe...  11.9 us
    another operation x2, other arithmetic, body(): jax.scipy.linalg.solve_triangular(lower_factor, identity, lower=True)  10.5 us
    dot_general x4, matrix products, body(): jnp.dot(square, start, precision=high, preferred_element_type=jnp.float32)  4.2 us

profile of v1, /device:TPU:1, one launch (start us, length us, event | category | flops | bytes accessed | tf_op | source)
XLA Modules:
  0.0 182.4 jit_solution(337886315942906203)
XLA Ops:
  0.6 12.9 %shard_map.41 = f32[3,256,256]{2,1,0:T(8,128)S(1)} custom-call(f32[8192,512]{1,0:T(8,128)} %x_ref.3), custom_call_target="tpu_custom_call" | custom-call | tf_op jit(solution)/shard_map/pallas_call | solution.py:49
  13.7 30.6 %all_to_all.10 = f32[128,12,128]{2,1,0:T(8,128)S(1)} all-to-all(f32[128,12,128]{2,1,0:T(8,128)S(1)} %reshape.23), channel_id=1, replica_groups=mesh['amp'=16,'blk'=8] {'amp','blk'}, dimensions={0} | all-to-all | bytes 1572864 | tf_op jit(solution)/shard_map/all_to_all | solution.py:91
  44.5 23.5 %all_to_all.11 = f32[128,12,128]{2,1,0:T(8,128)S(1)} all-to-all(f32[128,12,128]{2,1,0:T(8,128)S(1)} %broadcast_in_dim.2), channel_id=1, replica_groups=mesh['amp'=16,'blk'=8] {'amp','blk'}, dimensions={0} | all-to-all | bytes 1572864 | tf_op jit(solution)/shard_map/all_to_all | solution.py:94
  68.5 1.0 fusion.27
  69.5 0.6 fusion.28
  70.2 11.7 %cholesky.74 = f32[128,128]{1,0:T(8,128)S(1)} custom-call(f32[128,128]{1,0:T(8,128)S(1)} %add_multiply_fusion), custom_call_target="Cholesky" | custom-call | tf_op jit(solution)/shard_map/jit(cholesky)/cholesky | solution.py:99
  82.0 0.6 compare_reduce_fusion.3
  82.6 0.7 fusion.8
  83.3 9.8 %custom-call.13 = f32[1,128,128]{1,2,0:T(8,128)S(1)} custom-call(f32[1,128,128]{2,1,0:T(8,128)S(1)} %fusion.8), custom_call_target="InvertDiagBlocksLowerTriangular" | custom-call | tf_op jit(solution)/shard_map/jit(_solve_triangular)/triangular_solve | solution.py:100
  93.1 0.4 fusion.6
  93.5 1.0 fusion.26
  94.5 0.4 fusion.29
  95.0 11.9 %cholesky.85 = f32[128,128]{1,0:T(8,128)S(1)} custom-call(f32[128,128]{1,0:T(8,128)S(1)} %fusion.18), custom_call_target="Cholesky" | custom-call | tf_op jit(solution)/shard_map/jit(cholesky)/cholesky | solution.py:99
  107.0 0.6 compare_reduce_fusion.2
  107.6 0.7 fusion.9
  108.3 9.8 %custom-call.14 = f32[1,128,128]{1,2,0:T(8,128)S(1)} custom-call(f32[1,128,128]{2,1,0:T(8,128)S(1)} %fusion.9), custom_call_target="InvertDiagBlocksLowerTriangular" | custom-call | tf_op jit(solution)/shard_map/jit(_solve_triangular)/triangular_solve | solution.py:100
  118.1 0.4 fusion.4
  118.5 1.0 fusion.25
  120.0 11.7 %cholesky.96 = f32[128,128]{1,0:T(8,128)S(1)} custom-call(f32[128,128]{1,0:T(8,128)S(1)} %fusion.16), custom_call_target="Cholesky" | custom-call | tf_op jit(solution)/shard_map/jit(cholesky)/cholesky | solution.py:99
  131.8 0.6 compare_reduce_fusion.1
  132.4 0.7 fusion.10
  133.1 9.8 %custom-call.15 = f32[1,128,128]{1,2,0:T(8,128)S(1)} custom-call(f32[1,128,128]{2,1,0:T(8,128)S(1)} %fusion.10), custom_call_target="InvertDiagBlocksLowerTriangular" | custom-call | tf_op jit(solution)/shard_map/jit(_solve_triangular)/triangular_solve | solution.py:100
  142.9 0.4 fusion.2
  143.3 1.2 fusion.24
  145.1 11.7 %cholesky.107 = f32[128,128]{1,0:T(8,128)S(1)} custom-call(f32[128,128]{1,0:T(8,128)S(1)} %fusion.14), custom_call_target="Cholesky" | custom-call | tf_op jit(solution)/shard_map/jit(cholesky)/cholesky | solution.py:99
  156.8 0.6 compare_reduce_fusion
  157.4 0.7 fusion.11
  158.1 9.8 %custom-call.9 = f32[1,128,128]{1,2,0:T(8,128)S(1)} custom-call(f32[1,128,128]{2,1,0:T(8,128)S(1)} %fusion.11), custom_call_target="InvertDiagBlocksLowerTriangular" | custom-call | tf_op jit(solution)/shard_map/jit(_solve_triangular)/triangular_solve | solution.py:127
  167.9 0.4 fusion
  168.6 0.6 fusion.32.b_ref
  169.2 0.8 copy.15
  170.0 11.9 %shard_map.42 = f32[8192,128]{1,0:T(8,128)} custom-call(f32[8192,512]{1,0:T(8,128)} %x_ref.3, f32[512,128]{1,0:T(8,128)S(1)} %fusion.32.b_ref), custom_call_target="tpu_custom_call" | custom-call | tf_op jit(solution)/shard_map/pallas_call | solution.py:75
  (23 shorter events, 2.4 us)
Async XLA Ops:
  0.6 67.9 %copy-start = (f32[512,128]{1,0:T(8,128)S(1)}, f32[512,128]{1,0:T(8,128)}, u32[]{:S(2)}) copy-start(f32[512,128]{1,0:T(8,128)} %param.6) | copy-start | bytes 786436

commit v2 on v1

--- a/solution.py
+++ b/solution.py
@@ -1,3 +1,6 @@
+import functools
+import math
+
 import jax
 import jax.numpy as jnp
 from jax import lax
@@ -9,6 +12,7 @@
 AXES = ("amp", "blk")
 CHUNK = 1024
 HALF = 256
+SUB = 8
 
 
 def split(x):
@@ -95,37 +99,103 @@
     return pieces.reshape(blocks.shape)
 
 
-def factor(gram_block, cross_block):
-    lower_factor = jnp.linalg.cholesky(gram_block)
-    mixed = jax.scipy.linalg.solve_triangular(lower_factor, cross_block.T, lower=True).T
-    return (lower_factor, mixed)
+def contract(a, b, dims):
+    return lax.dot_general(
+        a, b, (dims, ((), ())), precision=lax.Precision.HIGHEST, preferred_element_type=jnp.float32
+    )
+
+
+def lanes(block, at):
+    return jnp.broadcast_to(block[:, at : at + 1], block.shape)
+
+
+def subs(block, at):
+    return jnp.broadcast_to(block[at : at + 1, :], block.shape)
+
+
+def inverse_factor(a):
+    n = a.shape[0]
+    blocks = n // SUB
+    row = lax.broadcasted_iota(jnp.int32, (SUB, n), 0)
+    col = lax.broadcasted_iota(jnp.int32, (SUB, n), 1)
+    left = [a[SUB * g : SUB * (g + 1), :] for g in range(blocks)]
+    right = [(col == row + SUB * g).astype(jnp.float32) for g in range(blocks)]
+    out = []
+    for b in range(blocks):
+        at = SUB * b
+        cols = [lanes(left[b], at + j) for j in range(SUB)]
+        s = {(i, j): subs(cols[j], i) for j in range(SUB) for i in range(j, SUB)}
+        ra = [subs(left[b], j) for j in range(SUB)]
+        rj = [subs(right[b], j) for j in range(SUB)]
+        inv, f = [], {}
+        for j in range(SUB):
+            inv.append(1.0 / s[j, j])
+            for i in range(j + 1, SUB):
+                f[i, j] = s[i, j] * inv[j]
+            for i in range(j + 1, SUB):
+                for l in range(j + 1, i + 1):
+                    s[i, l] = s[i, l] - f[i, j] * s[l, j]
+            for i in range(j + 1, SUB):
+                ra[i] = ra[i] - f[i, j] * ra[j]
+                rj[i] = rj[i] - f[i, j] * rj[j]
+        done = rj[SUB - 1] * lax.rsqrt(s[SUB - 1, SUB - 1])
+        for j in range(SUB - 1):
+            done = jnp.where(row == j, rj[j] * lax.rsqrt(s[j, j]), done)
+        out.append(done)
+        if b + 1 < blocks:
+            za = [ra[j] * inv[j] for j in range(SUB)]
+            zj = [rj[j] * inv[j] for j in range(SUB)]
+            for j in range(SUB - 1, -1, -1):
+                for i in range(j):
+                    za[i] = za[i] - f[j, i] * za[j]
+                    zj[i] = zj[i] - f[j, i] * zj[j]
+            for g in range(b + 1, blocks):
+                cols = [lanes(left[g], at + j) for j in range(SUB)]
+                for j in range(SUB):
+                    left[g] = left[g] - cols[j] * za[j]
+                    right[g] = right[g] - cols[j] * zj[j]
+    return jnp.concatenate(out, axis=0)
+
+
+def rounds_kernel(scale, g_ref, sketch_ref, matrix_ref, coef_ref, mixed_ref, start_ref, inv_ref):
+    mixed_ref[...] = sketch_ref[...]
+
+    def step(_, carry):
+        start = mixed_ref[...]
+        top, bottom = start[:HALF], start[HALF:]
+        cross_top = contract(g_ref[0], top, ((1,), (0,))) + contract(g_ref[1], bottom, ((1,), (0,)))
+        cross_bottom = contract(g_ref[1], top, ((0,), (0,))) + contract(g_ref[2], bottom, ((1,), (0,)))
+        gram_block = contract(top, cross_top, ((0,), (0,))) + contract(bottom, cross_bottom, ((0,), (0,)))
+        inv = inverse_factor(gram_block)
+        start_ref[...] = start
+        inv_ref[...] = inv
+        mixed_ref[:HALF] = contract(cross_top, inv, ((1,), (1,)))
+        mixed_ref[HALF:] = contract(cross_bottom, inv, ((1,), (1,)))
+        return carry
+
+    lax.fori_loop(0, POWER + 1, step, 0)
+    coef_ref[...] = mixed_ref[...] * (1.0 / scale)
+    matrix_ref[...] = contract(start_ref[...], inv_ref[...], ((1,), (1,))) * scale
+
+
+def rounds(blocks, sketch, scale):
+    frames, rank = sketch.shape
+    return pl.pallas_call(
+        functools.partial(rounds_kernel, scale),
+        out_shape=[jax.ShapeDtypeStruct((frames, rank), jnp.float32)] * 2,
+        scratch_shapes=[
+            pltpu.VMEM((frames, rank), jnp.float32),
+            pltpu.VMEM((frames, rank), jnp.float32),
+            pltpu.VMEM((rank, rank), jnp.float32),
+        ],
+        compiler_params=pltpu.CompilerParams(vmem_limit_bytes=48 * 2**20),
+    )(blocks, sketch)
 
 
 def body(pixels, sketch):
-    high = lax.Precision.HIGHEST
-    rank = sketch.shape[1]
     pixel_count = pixels.shape[0] * lax.axis_size("amp") * lax.axis_size("blk")
     summed = total(gram(pixels))
-    square = jnp.concatenate(
-        [
-            jnp.concatenate([summed[0], summed[1]], axis=1),
-            jnp.concatenate([summed[1].T, summed[2]], axis=1),
-        ],
-        axis=0,
-    )
-    mixed = sketch
-    lower_factor = None
-    start = None
-    for _ in range(POWER + 1):
-        start = mixed
-        cross_block = jnp.dot(square, start, precision=high, preferred_element_type=jnp.float32)
-        gram_block = jnp.dot(start.T, cross_block, precision=high, preferred_element_type=jnp.float32)
-        lower_factor, mixed = factor(gram_block, cross_block)
-    scale = jnp.sqrt(jnp.asarray(pixel_count, dtype=pixels.dtype))
-    coefficients = mixed / scale
-    identity = jnp.eye(rank, dtype=pixels.dtype)
-    inverse = jax.scipy.linalg.solve_triangular(lower_factor, identity, lower=True).T * scale
-    matrix = jnp.dot(start, inverse, precision=high, preferred_element_type=jnp.float32)
+    matrix, coefficients = rounds(summed, sketch, math.sqrt(pixel_count))
     return (apply_basis(pixels, matrix), coefficients)
 
 

time: 186 us -> 108 us (0.58); the launches traced: 182 us -> 108 us
  other arithmetic: 91.8 us -> 0.14 us
  Pallas kernels: 24.8 us -> 52.5 us
  matrix products: 8.46 us -> 0 us
    another operation x20 -> x0, other arithmetic: 91.6 us -> none  [the longest x12 49.7 us: factor(): lower_factor = jnp.linalg.cholesky(gram_block)]
    pallas_call x0 -> x1, Pallas kernels: none -> 27.6 us  [rounds(): pl.pallas_call(functools.partial(rounds_kernel, scale), out_shape=[jax.Sh...]
    dot_general x9 -> x0, matrix products: 6.54 us -> none  [the longest x4 4.2 us: body(): jnp.dot(square, start, precision=high, preferred_element_type=jnp.float32)]
    another operation x5 -> x0, matrix products: 1.92 us -> none  [the longest x4 1.66 us: factor(): jax.scipy.linalg.solve_triangular(lower_factor, cross_block.T, lower=True)]
where the time goes in v2:
time: 108 us
  blocking collectives  54.2 us (50%)
  Pallas kernels  52.5 us (49%)
    all_to_all x2, blocking collectives, total(): pieces = lax.all_to_all(pieces, AXES, 0, 0, tiled=True)  54.2 us
    pallas_call x1, Pallas kernels, rounds(): pl.pallas_call(functools.partial(rounds_kernel, scale), out_shape=[jax.Sh...  27.6 us
    pallas_call x1, Pallas kernels, gram(): pl.pallas_call(gram_kernel, grid=(rows // CHUNK,), in_specs=[pl.BlockSpec...  12.9 us
    pallas_call x1, Pallas kernels, apply_basis(): pl.pallas_call(basis_kernel, grid=(rows // CHUNK,), in_specs=[pl.BlockSpe...  11.9 us

profile of v2, /device:TPU:1, one launch (start us, length us, event | category | flops | bytes accessed | tf_op | source)
XLA Modules:
  0.0 107.9 jit_solution(11289649341096282107)
XLA Ops:
  0.6 0.0 copy-start
  0.6 12.9 %shard_map.41 = f32[3,256,256]{2,1,0:T(8,128)S(1)} custom-call(f32[8192,512]{1,0:T(8,128)} %x_ref.3), custom_call_target="tpu_custom_call" | custom-call | tf_op jit(solution)/shard_map/pallas_call | solution.py:53
  13.6 0.1 reshape.11
  13.7 30.7 %all_to_all.10 = f32[128,12,128]{2,1,0:T(8,128)S(1)} all-to-all(f32[128,12,128]{2,1,0:T(8,128)S(1)} %reshape.11), channel_id=1, replica_groups=mesh['amp'=16,'blk'=8] {'amp','blk'}, dimensions={0} | all-to-all | bytes 1572864 | tf_op jit(solution)/shard_map/all_to_all | solution.py:95
  44.3 0.1 reduce_sum.9
  44.5 0.1 broadcast_in_dim.2
  44.6 23.5 %all_to_all.11 = f32[128,12,128]{2,1,0:T(8,128)S(1)} all-to-all(f32[128,12,128]{2,1,0:T(8,128)S(1)} %broadcast_in_dim.2), channel_id=1, replica_groups=mesh['amp'=16,'blk'=8] {'amp','blk'}, dimensions={0} | all-to-all | bytes 1572864 | tf_op jit(solution)/shard_map/all_to_all | solution.py:98
  68.1 0.2 reshape.12.g_ref
  68.3 0.0 copy-done
  68.3 27.6 %shard_map.42 = (f32[512,128]{1,0:T(8,128)S(1)}, f32[512,128]{1,0:T(8,128)}) custom-call(f32[3,256,256]{2,1,0:T(8,128)S(1)} %reshape.12.g_ref, f32[512,128]{1,0:T(8,128)S(1)} %copy-done), custom_call_target="tpu_custom_call" | custom-call | tf_op jit(solution)/shard_map/pallas_call | solution.py:183
  95.9 11.9 %shard_map.43 = f32[8192,128]{1,0:T(8,128)} custom-call(f32[8192,512]{1,0:T(8,128)} %x_ref.3, f32[512,128]{1,0:T(8,128)S(1)} %get-tuple-element.4.b_ref), custom_call_target="tpu_custom_call" | custom-call | tf_op jit(solution)/shard_map/pallas_call | solution.py:79
Async XLA Ops:
  0.6 67.7 %copy-start = (f32[512,128]{1,0:T(8,128)S(1)}, f32[512,128]{1,0:T(8,128)}, u32[]{:S(2)}) copy-start(f32[512,128]{1,0:T(8,128)} %sketch_ref.1) | copy-start | bytes 786436

commit v3 on v2

--- a/solution.py
+++ b/solution.py
@@ -6,13 +6,17 @@
 from jax import lax
 from jax.experimental import pallas as pl
 from jax.experimental.pallas import tpu as pltpu
+from jax.sharding import Mesh
 from jax.sharding import PartitionSpec as P
 
 POWER = 3
-AXES = ("amp", "blk")
+AXES = ("y", "z", "x", "core")
+SIZES = (4, 4, 4, 2)
 CHUNK = 1024
 HALF = 256
 SUB = 8
+TILE = 128
+PAIRS = tuple((i, j) for i in range(4) for j in range(i, 4))
 
 
 def split(x):
@@ -43,9 +47,15 @@
     def _():
         hl = hl_ref[...]
         both = hl + hl.T
-        out_ref[0] = hh_ref[0] + both[:HALF, :HALF]
-        out_ref[1] = hh_ref[1] + both[:HALF, HALF:]
-        out_ref[2] = hh_ref[2] + both[HALF:, HALF:]
+        quarters = (
+            hh_ref[0] + both[:HALF, :HALF],
+            hh_ref[1] + both[:HALF, HALF:],
+            hh_ref[2] + both[HALF:, HALF:],
+        )
+        for at, (i, j) in enumerate(PAIRS):
+            quarter = quarters[i // 2 + j // 2]
+            r, c = TILE * (i % 2), TILE * (j % 2)
+            out_ref[TILE * at : TILE * (at + 1), :] = quarter[r : r + TILE, c : c + TILE]
 
 
 def gram(pixels):
@@ -54,8 +64,8 @@
         gram_kernel,
         grid=(rows // CHUNK,),
         in_specs=[pl.BlockSpec((CHUNK, frames), lambda i: (i, 0))],
-        out_specs=pl.BlockSpec((3, HALF, HALF), lambda i: (0, 0, 0)),
-        out_shape=jax.ShapeDtypeStruct((3, HALF, HALF), jnp.float32),
+        out_specs=pl.BlockSpec((TILE * len(PAIRS), TILE), lambda i: (0, 0)),
+        out_shape=jax.ShapeDtypeStruct((TILE * len(PAIRS), TILE), jnp.float32),
         scratch_shapes=[
             pltpu.VMEM((3, HALF, HALF), jnp.float32),
             pltpu.VMEM((frames, frames), jnp.float32),
@@ -89,14 +99,27 @@
     )(pixels, matrix)
 
 
-def total(blocks):
-    devices = lax.axis_size("amp") * lax.axis_size("blk")
-    pieces = blocks.reshape(devices, -1, 128)
-    pieces = lax.all_to_all(pieces, AXES, 0, 0, tiled=True)
-    piece = jnp.sum(pieces, axis=0)
-    pieces = jnp.broadcast_to(piece[None], (devices,) + piece.shape)
-    pieces = lax.all_to_all(pieces, AXES, 0, 0, tiled=True)
-    return pieces.reshape(blocks.shape)
+def all_to_all(pieces):
+    return lax.all_to_all(pieces, ("y", "x"), 0, 0, tiled=True)
+
+
+def swap(x, axis, bit):
+    return lax.ppermute(x, axis, [(i, i ^ bit) for i in range(lax.axis_size(axis))])
+
+
+def total(x):
+    core = lax.axis_index("core")
+    half = x.shape[0] // 2
+    mine = lax.dynamic_slice_in_dim(x, core * half, half, 0)
+    other = lax.dynamic_slice_in_dim(x, (1 - core) * half, half, 0)
+    mine = mine + swap(other, "core", 1)
+    group = lax.axis_size("y") * lax.axis_size("x")
+    piece = jnp.sum(all_to_all(mine.reshape(group, -1, x.shape[1])), axis=0)
+    for bit in (1, 3):
+        piece = piece + swap(piece, "z", bit)
+    mine = all_to_all(jnp.broadcast_to(piece[None], (group,) + piece.shape)).reshape(mine.shape)
+    other = swap(mine, "core", 1)
+    return jnp.where(core == 0, jnp.concatenate([mine, other]), jnp.concatenate([other, mine]))
 
 
 def contract(a, b, dims):
@@ -157,20 +180,22 @@
     return jnp.concatenate(out, axis=0)
 
 
-def rounds_kernel(scale, g_ref, sketch_ref, matrix_ref, coef_ref, mixed_ref, start_ref, inv_ref):
+def rounds_kernel(scale, blocks_ref, sketch_ref, matrix_ref, coef_ref, g_ref, mixed_ref, start_ref, inv_ref):
     mixed_ref[...] = sketch_ref[...]
+    for at, (i, j) in enumerate(PAIRS):
+        block = blocks_ref[TILE * at : TILE * (at + 1), :]
+        g_ref[TILE * i : TILE * (i + 1), TILE * j : TILE * (j + 1)] = block
+        if i != j:
+            g_ref[TILE * j : TILE * (j + 1), TILE * i : TILE * (i + 1)] = block.T
 
     def step(_, carry):
         start = mixed_ref[...]
-        top, bottom = start[:HALF], start[HALF:]
-        cross_top = contract(g_ref[0], top, ((1,), (0,))) + contract(g_ref[1], bottom, ((1,), (0,)))
-        cross_bottom = contract(g_ref[1], top, ((0,), (0,))) + contract(g_ref[2], bottom, ((1,), (0,)))
-        gram_block = contract(top, cross_top, ((0,), (0,))) + contract(bottom, cross_bottom, ((0,), (0,)))
+        cross_block = contract(g_ref[...], start, ((1,), (0,)))
+        gram_block = contract(start, cross_block, ((0,), (0,)))
         inv = inverse_factor(gram_block)
         start_ref[...] = start
         inv_ref[...] = inv
-        mixed_ref[:HALF] = contract(cross_top, inv, ((1,), (1,)))
-        mixed_ref[HALF:] = contract(cross_bottom, inv, ((1,), (1,)))
+        mixed_ref[...] = contract(cross_block, inv, ((1,), (1,)))
         return carry
 
     lax.fori_loop(0, POWER + 1, step, 0)
@@ -184,6 +209,7 @@
         functools.partial(rounds_kernel, scale),
         out_shape=[jax.ShapeDtypeStruct((frames, rank), jnp.float32)] * 2,
         scratch_shapes=[
+            pltpu.VMEM((frames, frames), jnp.float32),
             pltpu.VMEM((frames, rank), jnp.float32),
             pltpu.VMEM((frames, rank), jnp.float32),
             pltpu.VMEM((rank, rank), jnp.float32),
@@ -193,7 +219,7 @@
 
 
 def body(pixels, sketch):
-    pixel_count = pixels.shape[0] * lax.axis_size("amp") * lax.axis_size("blk")
+    pixel_count = pixels.shape[0] * math.prod(SIZES)
     summed = total(gram(pixels))
     matrix, coefficients = rounds(summed, sketch, math.sqrt(pixel_count))
     return (apply_basis(pixels, matrix), coefficients)
@@ -202,7 +228,7 @@
 def solution(mesh):
     return jax.shard_map(
         body,
-        mesh=mesh,
+        mesh=Mesh(mesh.devices.reshape(SIZES), AXES),
         in_specs=(P(AXES, None), P()),
         out_specs=(P(AXES, None), P()),
         check_vma=False,

time: 108 us -> 99.6 us (0.922)
  blocking collectives: 54.2 us -> 26.2 us
  starting transfers between devices: 0 us -> 11.5 us
  waiting for transfers between devices: 0 us -> 4.85 us
  Pallas kernels: 52.5 us -> 55.8 us
    all_to_all x2, blocking collectives: 54.2 us -> 26.2 us  [all_to_all(): return lax.all_to_all(pieces, ('y', 'x'), 0, 0, tiled=True)]
    ppermute x0 -> x4, starting transfers between devices: none -> 11.5 us  [swap(): lax.ppermute(x, axis, [(i, i ^ bit) for i in range(lax.axis_size(axis))])]
    ppermute x0 -> x4, waiting for transfers between devices: none -> 4.85 us  [swap(): lax.ppermute(x, axis, [(i, i ^ bit) for i in range(lax.axis_size(axis))])]
    pallas_call x1, Pallas kernels: 27.6 us -> 31 us  [rounds(): pl.pallas_call(functools.partial(rounds_kernel, scale), out_shape=[jax.Sh...]
  transfers between devices with their start and end apart: 0 -> 4, of which waited for: 0 -> 4; matrix products, arithmetic and copies ran while one was open for 0% -> 0% of each run, Pallas kernels for 0% -> 0%
where the time goes in v3:
time: 99.6 us; the launch traced here: 99.2 us
  Pallas kernels  55.8 us (56%)
  blocking collectives  26.2 us (26%)
  starting transfers between devices  11.5 us (12%)
  waiting for transfers between devices  4.85 us (5%)
    pallas_call x1, Pallas kernels, rounds(): pl.pallas_call(functools.partial(rounds_kernel, scale), out_shape=[jax.Sh...  31 us
    all_to_all x2, blocking collectives, all_to_all(): return lax.all_to_all(pieces, ('y', 'x'), 0, 0, tiled=True)  26.2 us
    pallas_call x1, Pallas kernels, gram(): pl.pallas_call(gram_kernel, grid=(rows // CHUNK,), in_specs=[pl.BlockSpec...  12.9 us
    pallas_call x1, Pallas kernels, apply_basis(): pl.pallas_call(basis_kernel, grid=(rows // CHUNK,), in_specs=[pl.BlockSpe...  11.9 us
    ppermute x4, starting transfers between devices, swap(): lax.ppermute(x, axis, [(i, i ^ bit) for i in range(lax.axis_size(axis))])  11.5 us
    ppermute x4, waiting for transfers between devices, swap(): lax.ppermute(x, axis, [(i, i ^ bit) for i in range(lax.axis_size(axis))])  4.85 us
  transfers between devices with their start and end apart: 4, of which 4 were waited for; matrix products, arithmetic and copies ran while one was open for 0% of the time, Pallas kernels for 0%

profile of v3, /device:TPU:1, one launch (start us, length us, event | category | flops | bytes accessed | tf_op | source)
XLA Modules:
  0.0 99.2 jit_solution(3165598898689734446)
XLA Ops:
  0.6 0.0 copy-start
  0.6 12.9 %shard_map.41 = f32[1280,128]{1,0:T(8,128)S(1)} custom-call(f32[8192,512]{1,0:T(8,128)} %x_ref.3), custom_call_target="tpu_custom_call" | custom-call | tf_op jit(solution)/shard_map/pallas_call | solution.py:63
  13.6 1.5 %collective-permute-start = (f32[640,128]{1,0:T(8,128)S(1)}, f32[640,128]{1,0:T(8,128)S(1)}, u32[]{:S(2)}, u32[]{:S(2)}) collective-permute-start(f32[640,128]{1,0:T(8,128)S(1)} %constant_dynamic-slice_fusion), channel_id=1, source_target_pairs={{0,1},{1,0},{2,3},{3,2},{4,5},{5,4},{6,7},{7,6},{8,9},{9,8},{10,11... | collective-permute-start | bytes 983048 | tf_op jit(solution)/shard_map/ppermute | solution.py:107
  15.0 1.3 %collective-permute-done = f32[640,128]{1,0:T(8,128)S(1)} collective-permute-done((f32[640,128]{1,0:T(8,128)S(1)}, f32[640,128]{1,0:T(8,128)S(1)}, u32[]{:S(2)}, u32[]{:S(2)}) %collective-permute-start) | collective-permute-done | bytes 327712 | tf_op jit(solution)/shard_map/ppermute | solution.py:107
  16.3 15.5 %all_to_all.10 = f32[16,40,128]{2,1,0:T(8,128)S(1)} all-to-all(f32[16,40,128]{2,1,0:T(8,128)S(1)} %bitcast.2), channel_id=1, replica_groups=mesh['y'=4,'z'=4,'x'=4,'core'=2] {'y','x'}, dimensions={0} | all-to-all | bytes 655360 | tf_op jit(solution)/shard_map/all_to_all | solution.py:103
  31.8 1.7 %collective-permute-start.1 = (f32[40,128]{1,0:T(8,128)S(1)}, f32[40,128]{1,0:T(8,128)S(1)}, u32[]{:S(2)}, u32[]{:S(2)}) collective-permute-start(f32[40,128]{1,0:T(8,128)S(1)} %reduce_sum.9), channel_id=1, source_target_pairs={{0,8},{8,0},{16,24},{24,16},{1,9},{9,1},{17,25},{25,17},{2,10},{10... | collective-permute-start | bytes 61448 | tf_op jit(solution)/shard_map/ppermute | solution.py:107
  33.6 1.2 %collective-permute-done.1 = f32[40,128]{1,0:T(8,128)S(1)} collective-permute-done((f32[40,128]{1,0:T(8,128)S(1)}, f32[40,128]{1,0:T(8,128)S(1)}, u32[]{:S(2)}, u32[]{:S(2)}) %collective-permute-start.1) | collective-permute-done | bytes 20512 | tf_op jit(solution)/shard_map/ppermute | solution.py:107
  34.7 3.6 %collective-permute-start.2 = (f32[40,128]{1,0:T(8,128)S(1)}, f32[40,128]{1,0:T(8,128)S(1)}, u32[]{:S(2)}, u32[]{:S(2)}) collective-permute-start(f32[40,128]{1,0:T(8,128)S(1)} %add.18), channel_id=1, source_target_pairs={{0,24},{8,16},{16,8},{24,0},{1,25},{9,17},{17,9},{25,1},{2,26},{10... | collective-permute-start | bytes 61448 | tf_op jit(solution)/shard_map/ppermute | solution.py:107
  38.3 1.2 %collective-permute-done.2 = f32[40,128]{1,0:T(8,128)S(1)} collective-permute-done((f32[40,128]{1,0:T(8,128)S(1)}, f32[40,128]{1,0:T(8,128)S(1)}, u32[]{:S(2)}, u32[]{:S(2)}) %collective-permute-start.2) | collective-permute-done | bytes 20512 | tf_op jit(solution)/shard_map/ppermute | solution.py:107
  39.5 10.7 %all_to_all.11 = f32[16,40,128]{2,1,0:T(8,128)S(1)} all-to-all(f32[16,40,128]{2,1,0:T(8,128)S(1)} %broadcast_in_dim.2), channel_id=1, replica_groups=mesh['y'=4,'z'=4,'x'=4,'core'=2] {'y','x'}, dimensions={0} | all-to-all | bytes 655360 | tf_op jit(solution)/shard_map/all_to_all | solution.py:103
  50.2 4.7 %collective-permute-start.3 = (f32[640,128]{1,0:T(8,128)S(1)}, f32[640,128]{1,0:T(8,128)S(1)}, u32[]{:S(2)}, u32[]{:S(2)}) collective-permute-start(f32[640,128]{1,0:T(8,128)S(1)} %bitcast.3), channel_id=1, source_target_pairs={{0,1},{1,0},{2,3},{3,2},{4,5},{5,4},{6,7},{7,6},{8,9},{9,8},{10,11... | collective-permute-start | bytes 983048 | tf_op jit(solution)/shard_map/ppermute | solution.py:107
  55.0 1.3 %collective-permute-done.3 = f32[640,128]{1,0:T(8,128)S(1)} collective-permute-done((f32[640,128]{1,0:T(8,128)S(1)}, f32[640,128]{1,0:T(8,128)S(1)}, u32[]{:S(2)}, u32[]{:S(2)}) %collective-permute-start.3) | collective-permute-done | bytes 327712 | tf_op jit(solution)/shard_map/ppermute | solution.py:107
  56.3 0.0 copy-done
  56.3 31.0 %shard_map.42 = (f32[512,128]{1,0:T(8,128)S(1)}, f32[512,128]{1,0:T(8,128)}) custom-call(f32[1280,128]{1,0:T(8,128)S(1)} %maximum_select_fusion.blocks_ref, f32[512,128]{1,0:T(8,128)S(1)} %copy-done), custom_call_target="tpu_custom_call" | custom-call | tf_op jit(solution)/shard_map/pallas_call | solution.py:208
  87.2 11.9 %shard_map.43 = f32[8192,128]{1,0:T(8,128)} custom-call(f32[8192,512]{1,0:T(8,128)} %x_ref.3, f32[512,128]{1,0:T(8,128)S(1)} %get-tuple-element.4.b_ref), custom_call_target="tpu_custom_call" | custom-call | tf_op jit(solution)/shard_map/pallas_call | solution.py:89
  (7 shorter events, 0.2 us)
Async XLA Ops:
  0.6 55.6 %copy-start = (f32[512,128]{1,0:T(8,128)S(1)}, f32[512,128]{1,0:T(8,128)}, u32[]{:S(2)}) copy-start(f32[512,128]{1,0:T(8,128)} %sketch_ref.1) | copy-start | bytes 786436
  13.6 2.7 %collective-permute-start = (f32[640,128]{1,0:T(8,128)S(1)}, f32[640,128]{1,0:T(8,128)S(1)}, u32[]{:S(2)}, u32[]{:S(2)}) collective-permute-start(f32[640,128]{1,0:T(8,128)S(1)} %constant_dynamic-slice_fusion), channel_id=1, source_target_pairs={{0,1},{1,0},{2,3},{3,2},{4,5},{5,4},{6,7},{7,6},{8,9},{9,8},{10,11... | collective-permute-start | bytes 983048 | tf_op jit(solution)/shard_map/ppermute | solution.py:107
  31.8 2.9 %collective-permute-start.1 = (f32[40,128]{1,0:T(8,128)S(1)}, f32[40,128]{1,0:T(8,128)S(1)}, u32[]{:S(2)}, u32[]{:S(2)}) collective-permute-start(f32[40,128]{1,0:T(8,128)S(1)} %reduce_sum.9), channel_id=1, source_target_pairs={{0,8},{8,0},{16,24},{24,16},{1,9},{9,1},{17,25},{25,17},{2,10},{10... | collective-permute-start | bytes 61448 | tf_op jit(solution)/shard_map/ppermute | solution.py:107
  34.7 4.7 %collective-permute-start.2 = (f32[40,128]{1,0:T(8,128)S(1)}, f32[40,128]{1,0:T(8,128)S(1)}, u32[]{:S(2)}, u32[]{:S(2)}) collective-permute-start(f32[40,128]{1,0:T(8,128)S(1)} %add.18), channel_id=1, source_target_pairs={{0,24},{8,16},{16,8},{24,0},{1,25},{9,17},{17,9},{25,1},{2,26},{10... | collective-permute-start | bytes 61448 | tf_op jit(solution)/shard_map/ppermute | solution.py:107
  50.2 6.0 %collective-permute-start.3 = (f32[640,128]{1,0:T(8,128)S(1)}, f32[640,128]{1,0:T(8,128)S(1)}, u32[]{:S(2)}, u32[]{:S(2)}) collective-permute-start(f32[640,128]{1,0:T(8,128)S(1)} %bitcast.3), channel_id=1, source_target_pairs={{0,1},{1,0},{2,3},{3,2},{4,5},{5,4},{6,7},{7,6},{8,9},{9,8},{10,11... | collective-permute-start | bytes 983048 | tf_op jit(solution)/shard_map/ppermute | solution.py:107

commit v4 on v3

v4 whole, which is shorter than its diff:
```python
import functools
import math

import jax
import jax.numpy as jnp
from jax import lax
from jax.experimental import pallas as pl
from jax.experimental.pallas import tpu as pltpu
from jax.sharding import Mesh
from jax.sharding import PartitionSpec as P

POWER = 3
AXES = ("y", "z", "x", "core")
SIZES = (4, 4, 4, 2)
CHUNK = 1024
HALF = 256
SUB = 8
AHEAD = 3
TILE = 128
PAIRS = tuple((i, j) for i in range(4) for j in range(i, 4))


def split(x):
    high = x.astype(jnp.bfloat16)
    return high, (x - high.astype(jnp.float32)).astype(jnp.bfloat16)


def dot_t(a, b):
    return lax.dot_general(a, b, (((0,), (0,)), ((), ())), preferred_element_type=jnp.float32)


def gram_kernel(x_ref, out_ref, hh_ref, hl_ref):
    step = pl.program_id(0)

    @pl.when(step == 0)
    def _():
        hh_ref[...] = jnp.zeros_like(hh_ref)
        hl_ref[...] = jnp.zeros_like(hl_ref)

    high, low = split(x_ref[...])
    left, right = high[:, :HALF], high[:, HALF:]
    hh_ref[0] += dot_t(left, left)
    hh_ref[1] += dot_t(left, right)
    hh_ref[2] += dot_t(right, right)
    hl_ref[...] += dot_t(high, low)

    @pl.when(step == pl.num_programs(0) - 1)
    def _():
        hl = hl_ref[...]
        both = hl + hl.T
        quarters = (
            hh_ref[0] + both[:HALF, :HALF],
            hh_ref[1] + both[:HALF, HALF:],
            hh_ref[2] + both[HALF:, HALF:],
        )
        for at, (i, j) in enumerate(PAIRS):
            quarter = quarters[i // 2 + j // 2]
            r, c = TILE * (i % 2), TILE * (j % 2)
            out_ref[TILE * at : TILE * (at + 1), :] = quarter[r : r + TILE, c : c + TILE]


def gram(pixels):
    rows, frames = pixels.shape
    return pl.pallas_call(
        gram_kernel,
        grid=(rows // CHUNK,),
        in_specs=[pl.BlockSpec((CHUNK, frames), lambda i: (i, 0))],
        out_specs=pl.BlockSpec((TILE * len(PAIRS), TILE), lambda i: (0, 0)),
        out_shape=jax.ShapeDtypeStruct((TILE * len(PAIRS), TILE), jnp.float32),
        scratch_shapes=[
            pltpu.VMEM((3, HALF, HALF), jnp.float32),
            pltpu.VMEM((frames, frames), jnp.float32),
        ],
        compiler_params=pltpu.CompilerParams(vmem_limit_bytes=48 * 2**20),
    )(pixels)


def all_to_all(pieces):
    return lax.all_to_all(pieces, ("y", "x"), 0, 0, tiled=True)


def swap(x, axis, bit):
    return lax.ppermute(x, axis, [(i, i ^ bit) for i in range(lax.axis_size(axis))])


def total(x):
    core = lax.axis_index("core")
    half = x.shape[0] // 2
    mine = lax.dynamic_slice_in_dim(x, core * half, half, 0)
    other = lax.dynamic_slice_in_dim(x, (1 - core) * half, half, 0)
    mine = mine + swap(other, "core", 1)
    group = lax.axis_size("y") * lax.axis_size("x")
    piece = jnp.sum(all_to_all(mine.reshape(group, -1, x.shape[1])), axis=0)
    for bit in (1, 3):
        piece = piece + swap(piece, "z", bit)
    mine = all_to_all(jnp.broadcast_to(piece[None], (group,) + piece.shape)).reshape(mine.shape)
    other = swap(mine, "core", 1)
    return jnp.where(core == 0, jnp.concatenate([mine, other]), jnp.concatenate([other, mine]))


def thirds(x):
    high = x.astype(jnp.bfloat16)
    rest = x - high.astype(jnp.float32)
    mid, low = split(rest)
    return high, mid, low


def contract(a, b, dims):
    return lax.dot_general(a, b, (dims, ((), ())), preferred_element_type=jnp.float32)


def lanes(block, at):
    return jnp.broadcast_to(block[:, at : at + 1], block.shape)


def rank_update(scaled, rows):
    h1, m1, l1 = (p.astype(jnp.float32) for p in thirds(scaled))
    h2, m2, l2 = (p.astype(jnp.float32) for p in thirds(rows))
    first = jnp.concatenate([h1, h1, m1, h1, m1, l1], axis=0).astype(jnp.bfloat16)
    second = jnp.concatenate([h2, m2, h2, l2, m2, h2], axis=0).astype(jnp.bfloat16)
    return contract(first, second, ((0,), (0,)))


def inverse_factor(a, buf_ref):
    n = a.shape[0]
    blocks = n // SUB
    row = lax.broadcasted_iota(jnp.int32, (SUB, n), 0)
    col = lax.broadcasted_iota(jnp.int32, (SUB, n), 1)
    rows = [a[SUB * g : SUB * (g + 1), :] for g in range(blocks)]
    out = []
    for b in range(blocks):
        at, slot = SUB * b, b % 2
        panel = (col >= at) & (col < at + SUB)
        own = rows[b]
        for j in range(SUB):
            buf_ref[slot, j] = lanes(own, at + j)
        s = {
            (i, j): jnp.broadcast_to(buf_ref[slot, j, i : i + 1, :], (SUB, n))
            for j in range(SUB)
            for i in range(j, SUB)
        }
        own = jnp.where(panel, (col == row + at).astype(jnp.float32), own)
        r = [jnp.broadcast_to(own[j : j + 1, :], own.shape) for j in range(SUB)]
        near = range(b + 1, min(b + 1 + AHEAD, blocks))
        columns = {}
        for g in near:
            columns[g] = [lanes(rows[g], at + j) for j in range(SUB)]
            rows[g] = jnp.where(panel, 0.0, rows[g])
        inv, f = [], {}
        for j in range(SUB):
            inv.append(1.0 / s[j, j])
            for i in range(j + 1, SUB):
                f[i, j] = s[i, j] * inv[j]
            for i in range(j + 1, SUB):
                for l in range(j + 1, i + 1):
                    s[i, l] = s[i, l] - f[i, j] * s[l, j]
            for i in range(j + 1, SUB):
                r[i] = r[i] - f[i, j] * r[j]
                for g in near:
                    columns[g][i] = columns[g][i] - f[i, j] * columns[g][j]
            for g in near:
                rows[g] = rows[g] - (columns[g][j] * inv[j]) * r[j]
        done, pivot, inverse = r[-1], s[SUB - 1, SUB - 1], inv[-1]
        for j in range(SUB - 1):
            done = jnp.where(row == j, r[j], done)
            pivot = jnp.where(row == j, s[j, j], pivot)
            inverse = jnp.where(row == j, inv[j], inverse)
        out.append(jnp.where(col < at + SUB, done * lax.rsqrt(pivot), 0.0))
        far = range(b + 1 + AHEAD, blocks)
        if far:
            update = rank_update(done * inverse, done)
            for g in far:
                rows[g] = jnp.where(panel, 0.0, rows[g]) - update[SUB * g : SUB * (g + 1), :]
    return jnp.concatenate(out, axis=0)


def times_inverse(x, inv):
    xh, xm, xl = thirds(x)
    ih, im, il = thirds(inv)
    first = jnp.concatenate([xh, xh, xm, xh, xl, xm], axis=1)
    second = jnp.concatenate([ih, im, ih, il, ih, im], axis=1)
    return contract(first, second, ((1,), (1,)))


def finish_kernel(
    scale, blocks_ref, sketch_ref, x_ref, basis_ref, coef_ref, g_ref, mixed_ref, start_ref, inv_ref, buf_ref,
    held_ref, done_ref, in_sems, out_sems,
):
    rows = x_ref.shape[0]
    chunks = rows // CHUNK

    def fetch(i):
        at = pl.ds(pl.multiple_of(i * CHUNK, CHUNK), CHUNK)
        return pltpu.make_async_copy(x_ref.at[at], held_ref.at[at], in_sems.at[i])

    def store(i):
        at = pl.ds(pl.multiple_of(i * CHUNK, CHUNK), CHUNK)
        return pltpu.make_async_copy(done_ref.at[at], basis_ref.at[at], out_sems.at[i])

    for i in range(chunks):
        fetch(i).start()

    frames, rank = sketch_ref.shape
    mixed_ref[...] = sketch_ref[...]
    for at, (i, j) in enumerate(PAIRS):
        block = blocks_ref[TILE * at : TILE * (at + 1), :]
        for p, q in ((i, j), (j, i))[: 1 if i == j else 2]:
            part = thirds(block if (p, q) == (i, j) else block.T)
            for k in range(3):
                g_ref[TILE * p : TILE * (p + 1), k * frames + TILE * q : k * frames + TILE * (q + 1)] = part[k]

    def step(_, carry):
        start = mixed_ref[...]
        sh, sm, sl = thirds(start)
        pair = jnp.concatenate([sh, sm], axis=1)
        high = contract(g_ref[:, :frames], pair, ((1,), (0,)))
        mid = contract(g_ref[:, frames : 2 * frames], pair, ((1,), (0,)))
        small = contract(g_ref[:, :frames], sl, ((1,), (0,))) + contract(g_ref[:, 2 * frames :], sh, ((1,), (0,)))
        cross = high[:, :rank] + ((high[:, rank:] + mid[:, :rank]) + (mid[:, rank:] + small))
        ch, cm, cl = thirds(cross)
        square = contract(pair, jnp.concatenate([ch, cm], axis=1), ((0,), (0,)))
        small = contract(sh, cl, ((0,), (0,))) + contract(sl, ch, ((0,), (0,)))
        gram_block = square[:rank, :rank] + (
            (square[:rank, rank:] + square[rank:, :rank]) + (square[rank:, rank:] + small)
        )
        inv = inverse_factor(gram_block, buf_ref)
        start_ref[...] = start
        inv_ref[...] = inv
        mixed_ref[...] = times_inverse(cross, inv)
        return carry

    lax.fori_loop(0, POWER + 1, step, 0)
    coef_ref[...] = mixed_ref[...] * (1.0 / scale)
    b_high, b_low = split(times_inverse(start_ref[...], inv_ref[...]) * scale)
    both = jnp.concatenate([b_high, b_low], axis=1)

    def apply(i, carry):
        fetch(i).wait()
        at = pl.ds(pl.multiple_of(i * CHUNK, CHUNK), CHUNK)
        high, low = split(held_ref[at, :])
        wide = contract(high, both, ((1,), (0,)))
        done_ref[at, :] = wide[:, :rank] + (wide[:, rank:] + contract(low, b_high, ((1,), (0,))))
        store(i).start()
        return carry

    lax.fori_loop(0, chunks, apply, 0)
    for i in range(chunks):
        store(i).wait()


def finish(blocks, sketch, pixels, scale):
    frames, rank = sketch.shape
    rows = pixels.shape[0]
    whole = pl.BlockSpec(memory_space=pltpu.VMEM)
    outside = pl.BlockSpec(memory_space=pl.ANY)
    return pl.pallas_call(
        functools.partial(finish_kernel, scale),
        in_specs=[whole, whole, outside],
        out_specs=[outside, whole],
        out_shape=[
            jax.ShapeDtypeStruct((rows, rank), jnp.float32),
            jax.ShapeDtypeStruct((frames, rank), jnp.float32),
        ],
        scratch_shapes=[
            pltpu.VMEM((frames, 3 * frames), jnp.bfloat16),
            pltpu.VMEM((frames, rank), jnp.float32),
            pltpu.VMEM((frames, rank), jnp.float32),
            pltpu.VMEM((rank, rank), jnp.float32),
            pltpu.VMEM((2, SUB, SUB, rank), jnp.float32),
            pltpu.VMEM((rows, frames), jnp.float32),
            pltpu.VMEM((rows, rank), jnp.float32),
            pltpu.SemaphoreType.DMA((rows // CHUNK,)),
            pltpu.SemaphoreType.DMA((rows // CHUNK,)),
        ],
        compiler_params=pltpu.CompilerParams(vmem_limit_bytes=48 * 2**20),
    )(blocks, sketch, pixels)


def body(pixels, sketch):
    pixel_count = pixels.shape[0] * math.prod(SIZES)
    summed = total(gram(pixels))
    return finish(summed, sketch, pixels, math.sqrt(pixel_count))


def solution(mesh):
    return jax.shard_map(
        body,
        mesh=Mesh(mesh.devices.reshape(SIZES), AXES),
        in_specs=(P(AXES, None), P()),
        out_specs=(P(AXES, None), P()),
        check_vma=False,
    )
```

time: 99.6 us -> 84.9 us (0.85)
  Pallas kernels: 55.8 us -> 41.2 us
    pallas_call x2 -> x1, Pallas kernels: 42.9 us -> 28.3 us  [finish(): pl.pallas_call(functools.partial(finish_kernel, scale), in_specs=[whole,...]
where the time goes in v4:
time: 84.9 us; the launch traced here: 84.6 us
  Pallas kernels  41.2 us (49%)
  blocking collectives  26.2 us (31%)
  starting transfers between devices  11.5 us (14%)
  waiting for transfers between devices  4.85 us (6%)
    pallas_call x1, Pallas kernels, finish(): pl.pallas_call(functools.partial(finish_kernel, scale), in_specs=[whole,...  28.3 us
    all_to_all x2, blocking collectives, all_to_all(): return lax.all_to_all(pieces, ('y', 'x'), 0, 0, tiled=True)  26.2 us
    pallas_call x1, Pallas kernels, gram(): pl.pallas_call(gram_kernel, grid=(rows // CHUNK,), in_specs=[pl.BlockSpec...  12.9 us
    ppermute x4, starting transfers between devices, swap(): lax.ppermute(x, axis, [(i, i ^ bit) for i in range(lax.axis_size(axis))])  11.5 us
    ppermute x4, waiting for transfers between devices, swap(): lax.ppermute(x, axis, [(i, i ^ bit) for i in range(lax.axis_size(axis))])  4.85 us
  transfers between devices with their start and end apart: 4, of which 4 were waited for; matrix products, arithmetic and copies ran while one was open for 0% of the time, Pallas kernels for 0%

profile of v4, /device:TPU:1, one launch (start us, length us, event | category | flops | bytes accessed | tf_op | source)
XLA Modules:
  0.0 84.6 jit_solution(10236369807736347879)
XLA Ops:
  0.6 0.0 copy-start
  0.6 12.9 %shard_map.41 = f32[1280,128]{1,0:T(8,128)S(1)} custom-call(f32[8192,512]{1,0:T(8,128)} %x_ref.3), custom_call_target="tpu_custom_call" | custom-call | tf_op jit(solution)/shard_map/pallas_call | solution.py:64
  13.6 1.5 %collective-permute-start = (f32[640,128]{1,0:T(8,128)S(1)}, f32[640,128]{1,0:T(8,128)S(1)}, u32[]{:S(2)}, u32[]{:S(2)}) collective-permute-start(f32[640,128]{1,0:T(8,128)S(1)} %constant_dynamic-slice_fusion), channel_id=1, source_target_pairs={{0,1},{1,0},{2,3},{3,2},{4,5},{5,4},{6,7},{7,6},{8,9},{9,8},{10,11... | collective-permute-start | bytes 983048 | tf_op jit(solution)/shard_map/ppermute | solution.py:83
  15.0 1.3 %collective-permute-done = f32[640,128]{1,0:T(8,128)S(1)} collective-permute-done((f32[640,128]{1,0:T(8,128)S(1)}, f32[640,128]{1,0:T(8,128)S(1)}, u32[]{:S(2)}, u32[]{:S(2)}) %collective-permute-start) | collective-permute-done | bytes 327712 | tf_op jit(solution)/shard_map/ppermute | solution.py:83
  16.3 15.5 %all_to_all.10 = f32[16,40,128]{2,1,0:T(8,128)S(1)} all-to-all(f32[16,40,128]{2,1,0:T(8,128)S(1)} %bitcast.2), channel_id=1, replica_groups=mesh['y'=4,'z'=4,'x'=4,'core'=2] {'y','x'}, dimensions={0} | all-to-all | bytes 655360 | tf_op jit(solution)/shard_map/all_to_all | solution.py:79
  31.8 1.7 %collective-permute-start.1 = (f32[40,128]{1,0:T(8,128)S(1)}, f32[40,128]{1,0:T(8,128)S(1)}, u32[]{:S(2)}, u32[]{:S(2)}) collective-permute-start(f32[40,128]{1,0:T(8,128)S(1)} %reduce_sum.9), channel_id=1, source_target_pairs={{0,8},{8,0},{16,24},{24,16},{1,9},{9,1},{17,25},{25,17},{2,10},{10... | collective-permute-start | bytes 61448 | tf_op jit(solution)/shard_map/ppermute | solution.py:83
  33.6 1.2 %collective-permute-done.1 = f32[40,128]{1,0:T(8,128)S(1)} collective-permute-done((f32[40,128]{1,0:T(8,128)S(1)}, f32[40,128]{1,0:T(8,128)S(1)}, u32[]{:S(2)}, u32[]{:S(2)}) %collective-permute-start.1) | collective-permute-done | bytes 20512 | tf_op jit(solution)/shard_map/ppermute | solution.py:83
  34.7 3.6 %collective-permute-start.2 = (f32[40,128]{1,0:T(8,128)S(1)}, f32[40,128]{1,0:T(8,128)S(1)}, u32[]{:S(2)}, u32[]{:S(2)}) collective-permute-start(f32[40,128]{1,0:T(8,128)S(1)} %add.18), channel_id=1, source_target_pairs={{0,24},{8,16},{16,8},{24,0},{1,25},{9,17},{17,9},{25,1},{2,26},{10... | collective-permute-start | bytes 61448 | tf_op jit(solution)/shard_map/ppermute | solution.py:83
  38.3 1.2 %collective-permute-done.2 = f32[40,128]{1,0:T(8,128)S(1)} collective-permute-done((f32[40,128]{1,0:T(8,128)S(1)}, f32[40,128]{1,0:T(8,128)S(1)}, u32[]{:S(2)}, u32[]{:S(2)}) %collective-permute-start.2) | collective-permute-done | bytes 20512 | tf_op jit(solution)/shard_map/ppermute | solution.py:83
  39.5 10.7 %all_to_all.11 = f32[16,40,128]{2,1,0:T(8,128)S(1)} all-to-all(f32[16,40,128]{2,1,0:T(8,128)S(1)} %broadcast_in_dim.2), channel_id=1, replica_groups=mesh['y'=4,'z'=4,'x'=4,'core'=2] {'y','x'}, dimensions={0} | all-to-all | bytes 655360 | tf_op jit(solution)/shard_map/all_to_all | solution.py:79
  50.2 4.7 %collective-permute-start.3 = (f32[640,128]{1,0:T(8,128)S(1)}, f32[640,128]{1,0:T(8,128)S(1)}, u32[]{:S(2)}, u32[]{:S(2)}) collective-permute-start(f32[640,128]{1,0:T(8,128)S(1)} %bitcast.3), channel_id=1, source_target_pairs={{0,1},{1,0},{2,3},{3,2},{4,5},{5,4},{6,7},{7,6},{8,9},{9,8},{10,11... | collective-permute-start | bytes 983048 | tf_op jit(solution)/shard_map/ppermute | solution.py:83
  55.0 1.3 %collective-permute-done.3 = f32[640,128]{1,0:T(8,128)S(1)} collective-permute-done((f32[640,128]{1,0:T(8,128)S(1)}, f32[640,128]{1,0:T(8,128)S(1)}, u32[]{:S(2)}, u32[]{:S(2)}) %collective-permute-start.3) | collective-permute-done | bytes 327712 | tf_op jit(solution)/shard_map/ppermute | solution.py:83
  56.3 0.0 copy-done
  56.3 28.3 %shard_map.42 = (f32[8192,128]{1,0:T(8,128)}, f32[512,128]{1,0:T(8,128)}) custom-call(f32[1280,128]{1,0:T(8,128)S(1)} %maximum_select_fusion.blocks_ref, f32[512,128]{1,0:T(8,128)S(1)} %copy-done, f32[8192,512]{1,0:T(8,128)} %x_ref.3), custom_call_target="tpu_custom_call" | custom-call | tf_op jit(solution)/shard_map/pallas_call | solution.py:256
  (7 shorter events, 0.2 us)
Async XLA Ops:
  0.6 55.6 %copy-start = (f32[512,128]{1,0:T(8,128)S(1)}, f32[512,128]{1,0:T(8,128)}, u32[]{:S(2)}) copy-start(f32[512,128]{1,0:T(8,128)} %sketch_ref.1) | copy-start | bytes 786436
  13.6 2.7 %collective-permute-start = (f32[640,128]{1,0:T(8,128)S(1)}, f32[640,128]{1,0:T(8,128)S(1)}, u32[]{:S(2)}, u32[]{:S(2)}) collective-permute-start(f32[640,128]{1,0:T(8,128)S(1)} %constant_dynamic-slice_fusion), channel_id=1, source_target_pairs={{0,1},{1,0},{2,3},{3,2},{4,5},{5,4},{6,7},{7,6},{8,9},{9,8},{10,11... | collective-permute-start | bytes 983048 | tf_op jit(solution)/shard_map/ppermute | solution.py:83
  31.8 2.9 %collective-permute-start.1 = (f32[40,128]{1,0:T(8,128)S(1)}, f32[40,128]{1,0:T(8,128)S(1)}, u32[]{:S(2)}, u32[]{:S(2)}) collective-permute-start(f32[40,128]{1,0:T(8,128)S(1)} %reduce_sum.9), channel_id=1, source_target_pairs={{0,8},{8,0},{16,24},{24,16},{1,9},{9,1},{17,25},{25,17},{2,10},{10... | collective-permute-start | bytes 61448 | tf_op jit(solution)/shard_map/ppermute | solution.py:83
  34.7 4.7 %collective-permute-start.2 = (f32[40,128]{1,0:T(8,128)S(1)}, f32[40,128]{1,0:T(8,128)S(1)}, u32[]{:S(2)}, u32[]{:S(2)}) collective-permute-start(f32[40,128]{1,0:T(8,128)S(1)} %add.18), channel_id=1, source_target_pairs={{0,24},{8,16},{16,8},{24,0},{1,25},{9,17},{17,9},{25,1},{2,26},{10... | collective-permute-start | bytes 61448 | tf_op jit(solution)/shard_map/ppermute | solution.py:83
  50.2 6.0 %collective-permute-start.3 = (f32[640,128]{1,0:T(8,128)S(1)}, f32[640,128]{1,0:T(8,128)S(1)}, u32[]{:S(2)}, u32[]{:S(2)}) collective-permute-start(f32[640,128]{1,0:T(8,128)S(1)} %bitcast.3), channel_id=1, source_target_pairs={{0,1},{1,0},{2,3},{3,2},{4,5},{5,4},{6,7},{7,6},{8,9},{9,8},{10,11... | collective-permute-start | bytes 983048 | tf_op jit(solution)/shard_map/ppermute | solution.py:83
